TPU v7x, 32 devices: a whole 2x2x4 slice. The times are simulated.
32 devices in a mesh: grp: 2 (over y), zone: 4 (over x, core), tile: 4 (over z).
Axes of the slice: x: 2, y: 2, z: 4, core: 2. Of those that a mesh axis runs over, the one named last changes fastest.
Arguments:
- mask_levels: int32 [8, 512, 512], P(('grp', 'tile')), parts along dimension 0, may hold values from 0 to 15
- blend_weights: int32 [8, 512], P(('grp', 'tile')), parts along dimension 0, may hold values from 0 to 16
- zone_pairs: int32 [8, 2], P('grp'), parts along dimension 0, may hold values from 0 to 3, as said below
- kernels: bfloat16 [4, 4, 2, 512, 512], P(None, 'zone', None, 'tile'), may hold values from -6 to 6
- resist_cot: float32 [8, 512, 512], P(('grp', 'tile')), parts along dimension 0, may hold values from -6 to 6
Outputs:
- mask_grad: float32 [8, 512, 512], P(('grp', 'tile'), 'zone'), parts along dimension 0
- kernel_grad: float32 [8, 4, 2, 512, 512], P('grp', 'zone', None, 'tile'), parts along dimension 0
There are 2 independent parts, one for each index of `grp`. A program takes and returns all parts, laid end to end along the dimension named above; an argument that names none is the same for every part. Nothing has to cross between parts.
Inputs may be any that keep to these rules, and one draw needn't show every extreme that they name: `zone_pairs`: column 0 lists the 4 zones in some order, each once; in each row, column 1 is either the same zone as column 0 or the next zone after it, where the zone after zone 3 is zone 0.
All inputs are finite; a program needn't handle non-finite values.
Results may differ from a plain program's by a relative error of at most 0.017.
The roundings to bfloat16 on the way count: a program that leaves them out, or rounds other values in their place, can miss the bound.
Values may be sent and summed in bfloat16 or wider, within the bound.
A program may use at most 128 MiB of HBM per device.

v0:
```python
import functools
import math

import jax
import jax.numpy as jnp
import ml_dtypes
import numpy as np
from jax import lax
from jax.experimental import pallas as pl
from jax.experimental.pallas import tpu as pltpu
from jax.sharding import PartitionSpec as P

LEVELS = 15
BLEND = 16
STEEP = 4.0
THRESHOLD = 1.0
F32 = jnp.float32
BF16 = jnp.bfloat16
MESH = pl.DeviceIdType.MESH
CORES = 2


def stacked_tables(length):
    index = np.arange(length, dtype=np.int64)
    angle = ((index[:, None] * index[None, :]) % length) * (2.0 * math.pi / length)
    factor = 1.0 / math.sqrt(length)
    cos = (np.cos(angle) * factor).astype(np.float32).astype(ml_dtypes.bfloat16)
    sin = (-np.sin(angle) * factor).astype(np.float32).astype(ml_dtypes.bfloat16)
    back = np.block([[cos, sin], [-sin, cos]]).astype(ml_dtypes.bfloat16)
    fore = np.block([[cos, -sin], [sin, cos]]).astype(ml_dtypes.bfloat16)
    return back, fore


def dot(left, right):
    return jnp.dot(left, right, preferred_element_type=F32)


def blocks(total, step, body):
    def one(index, carry):
        body(pl.multiple_of(index * step, step))
        return carry

    lax.fori_loop(0, total // step, one, 0)


def kernel(
    sizes,
    pairs,
    blend,
    kern,
    levels_any,
    cot_any,
    back_any,
    fore_any,
    mask_out,
    kgrad_out,
    levels,
    cot,
    back,
    fore,
    outgoing,
    panels,
    mvals,
    left,
    spec,
    wave,
    fields,
    image,
    sib_in,
    chip_sum,
    chip_in,
    slope,
    kg_send,
    kg_recv,
    ygrad,
    ystack,
    mk_own,
    mk_send,
    mk_recv,
    local_sem,
    pan_s,
    pan_r,
    sib_s,
    sib_r,
    chip_s,
    chip_r,
    slope_s,
    slope_r,
    kg_s,
    kg_r,
    mk_s,
    mk_r,
):
    tiles, zdev, length, rows, zones = sizes
    n = length
    step = n // 2
    zrows = n // zdev
    chips = zdev // CORES
    me_t = lax.axis_index("tile")
    me_z = lax.axis_index("zone")
    chip = me_z // CORES
    core = me_z % CORES
    sib = chip * CORES + (1 - core)

    loads = [
        pltpu.make_async_copy(src, dst, local_sem.at[i])
        for i, (src, dst) in enumerate(
            ((levels_any, levels), (back_any, back), (fore_any, fore), (cot_any, cot))
        )
    ]
    barrier = pltpu.get_barrier_semaphore()
    for d in range(1, tiles):
        pl.semaphore_signal(
            barrier, inc=1, device_id={"tile": lax.rem(me_t + d, tiles)}, device_id_type=MESH
        )
    for d in range(1, zdev):
        pl.semaphore_signal(
            barrier, inc=1, device_id={"zone": lax.rem(me_z + d, zdev)}, device_id_type=MESH
        )
    my_rows = pl.ds(pl.multiple_of(me_t * rows, rows), rows)
    for t in range(tiles):
        for s in range(2):
            outgoing[t, s] = kern[pairs[t, s], 0]
    for s in range(2):
        panels[s, :, my_rows, :] = kern[pairs[me_t, s], 0]
    pl.semaphore_wait(barrier, tiles + zdev - 2)

    def panel_copy(s, d):
        peer = lax.rem(me_t + d, tiles)
        return pltpu.make_async_remote_copy(
            src_ref=outgoing.at[peer, s],
            dst_ref=panels.at[s, :, my_rows, :],
            send_sem=pan_s.at[s, d - 1],
            recv_sem=pan_r.at[s, d - 1],
            device_id={"tile": peer},
            device_id_type=MESH,
        )

    for s in range(2):
        for d in range(tiles - 1, 0, -1):
            panel_copy(s, d).start()
    for load in loads:
        load.start()

    first_zone, second_zone = pairs[me_t, 0], pairs[me_t, 1]
    share0 = jnp.where(first_zone != second_zone, blend[...].astype(F32) / BLEND, F32(1.0))
    shares = (share0, 1.0 - share0)

    loads[0].wait()
    mvals[...] = (2.0 * levels[...].astype(F32) / LEVELS - 1.0).astype(BF16)
    loads[1].wait()
    loads[2].wait()
    for h in range(2):

        def stage(r, h=h):
            left[pl.ds(r, step), h * n : (h + 1) * n] = dot(
                fore[pl.ds(h * n + r, step), :n], mvals[...]
            ).astype(BF16)

        blocks(n, step, stage)

    def stage(r):
        spec[pl.ds(r, step), :] = dot(left[pl.ds(r, step), :], back[...])

    blocks(n, step, stage)

    def from_left(table, h):
        def stage(r):
            left[pl.ds(r, step), h * n : (h + 1) * n] = dot(
                table[pl.ds(h * n + r, step), :], wave[...]
            ).astype(BF16)

        blocks(n, step, stage)

    for s in range(2):
        for d in range(1, tiles):
            panel_copy(s, d).wait_recv()

        def stage(r, s=s):
            at = pl.ds(r, 64)
            hr, hi = panels[s, 0, at, :].astype(F32), panels[s, 1, at, :].astype(F32)
            sr, si = spec[at, :n], spec[at, n:]
            wave[at, :] = (hr * sr - hi * si).astype(BF16)
            wave[pl.ds(n + r, 64), :] = (hr * si + hi * sr).astype(BF16)

        blocks(n, 64, stage)
        from_left(back, 0)
        from_left(back, 1)

        def stage(r, s=s):
            at = pl.ds(r, step)
            e = dot(left[at, :], fore[...])
            fields[s, at, :] = e
            er, ei = e[:, :n], e[:, n:]
            term = shares[s] * (er * er + ei * ei)
            image[at, :] = term if s == 0 else image[at, :] + term

        blocks(n, step, stage)

    half = n // CORES
    mine = pl.ds(pl.multiple_of(core * half, half), half)
    other = pl.ds(pl.multiple_of((1 - core) * half, half), half)
    to_sib = pltpu.make_async_remote_copy(
        src_ref=image.at[other, :],
        dst_ref=sib_in,
        send_sem=sib_s,
        recv_sem=sib_r,
        device_id={"zone": sib},
        device_id_type=MESH,
    )
    to_sib.start()
    to_sib.wait_recv()
    chip_sum[...] = image[mine, :] + sib_in[...]

    def chip_copy(d):
        return pltpu.make_async_remote_copy(
            src_ref=chip_sum,
            dst_ref=chip_in.at[d - 1],
            send_sem=chip_s.at[d - 1],
            recv_sem=chip_r.at[d - 1],
            device_id={"zone": lax.rem(chip + d, chips) * CORES + core},
            device_id_type=MESH,
        )

    for d in range(1, chips):
        chip_copy(d).start()
    loads[3].wait()
    for d in range(1, chips):
        chip_copy(d).wait_recv()

    def stage(r):
        at = pl.ds(r, 64)
        total = chip_sum[at, :]
        for d in range(1, chips):
            total = total + chip_in[d - 1, at, :]
        resist = jax.nn.sigmoid(STEEP * (total - THRESHOLD))
        here = pl.ds(pl.multiple_of(core * half + r, 64), 64)
        slope[here, :] = cot[here, :] * STEEP * resist * (1.0 - resist)

    blocks(half, 64, stage)
    slope_copy = pltpu.make_async_remote_copy(
        src_ref=slope.at[mine, :],
        dst_ref=slope.at[mine, :],
        send_sem=slope_s,
        recv_sem=slope_r,
        device_id={"zone": sib},
        device_id_type=MESH,
    )
    slope_copy.start()
    slope_copy.wait_recv()

    def kg_copy(s, d):
        peer = lax.rem(me_t + d, tiles)
        return pltpu.make_async_remote_copy(
            src_ref=kg_send.at[peer, s],
            dst_ref=kg_recv.at[me_t, s],
            send_sem=kg_s.at[s, d - 1],
            recv_sem=kg_r.at[s, d - 1],
            device_id={"tile": peer},
            device_id_type=MESH,
        )

    for s in range(2):

        def stage(r, s=s):
            at = pl.ds(r, 64)
            scaled = 2.0 * shares[s] * slope[at, :]
            wave[at, :] = (scaled * fields[s, at, :n]).astype(BF16)
            wave[pl.ds(n + r, 64), :] = (scaled * fields[s, at, n:]).astype(BF16)

        blocks(n, 64, stage)
        from_left(fore, 0)
        from_left(fore, 1)

        def rows_of(peer, s=s):
            base = pl.multiple_of(peer * rows, rows)
            at = pl.ds(base, rows)
            v = dot(left[at, :], back[...])
            vr, vi = v[:, :n], v[:, n:]
            sr, si = spec[at, :n], spec[at, n:]
            hr, hi = panels[s, 0, at, :].astype(F32), panels[s, 1, at, :].astype(F32)
            yr = vr * hr + vi * hi
            yi = vi * hr - vr * hi
            if s == 0:
                ygrad[at, :n] = yr
                ygrad[at, n:] = yi
            else:
                ystack[at, :] = (ygrad[at, :n] + yr).astype(BF16)
                ystack[pl.ds(n + base, rows), :] = (ygrad[at, n:] + yi).astype(BF16)
            return (vr * sr + vi * si).astype(BF16), (vi * sr - vr * si).astype(BF16)

        def away(i, carry, s=s):
            d = tiles - 1 - i
            peer = lax.rem(me_t + d, tiles)
            re, im = rows_of(peer)
            kg_send[peer, s, 0] = re
            kg_send[peer, s, 1] = im
            kg_copy(s, d).start()
            return carry

        lax.fori_loop(0, tiles - 1, away, 0)
        re, im = rows_of(me_t)
        kg_recv[me_t, s, 0] = re
        kg_recv[me_t, s, 1] = im

    for h in range(2):

        def stage(r, h=h):
            left[pl.ds(r, step), h * n : (h + 1) * n] = dot(
                back[pl.ds(h * n + r, step), :], ystack[...]
            ).astype(BF16)

        blocks(n, step, stage)

    def mk_copy(d):
        peer = lax.rem(me_z + d, zdev)
        return pltpu.make_async_remote_copy(
            src_ref=mk_send.at[peer],
            dst_ref=mk_recv.at[d - 1],
            send_sem=mk_s.at[d - 1],
            recv_sem=mk_r.at[d - 1],
            device_id={"zone": peer},
            device_id_type=MESH,
        )

    def mask_rows(peer):
        return dot(left[pl.ds(pl.multiple_of(peer * zrows, zrows), zrows), :], fore[:, :n])

    def away(i, carry):
        d = i + 1
        peer = lax.rem(me_z + d, zdev)
        mk_send[peer] = mask_rows(peer).astype(BF16)
        mk_copy(d).start()
        return carry

    lax.fori_loop(0, zdev - 1, away, 0)
    mk_own[...] = mask_rows(me_z)
    total = mk_own[...]
    for d in range(1, zdev):
        mk_copy(d).wait_recv()
        total = total + mk_recv[d - 1].astype(F32)
    mask_out[...] = total

    owners = []
    for z in range(zones):
        owner = jnp.int32(0)
        for t in range(tiles):
            owner = jnp.where(pairs[t, 0] == z, jnp.int32(t), owner)
        owners.append(owner)
    for s in range(2):
        for d in range(1, tiles):
            kg_copy(s, d).wait_recv()
    for z in range(zones):
        own, prior = owners[z], owners[(z - 1) % zones]
        keep_own = pairs[own, 1] == pairs[own, 0]
        keep_prior = pairs[prior, 1] != pairs[prior, 0]
        value = kg_recv[own, 0].astype(F32)
        value = value + jnp.where(keep_own, kg_recv[own, 1].astype(F32), 0.0)
        value = value + jnp.where(keep_prior, kg_recv[prior, 1].astype(F32), 0.0)
        kgrad_out[z, 0] = value

    for s in range(2):
        for d in range(1, tiles):
            panel_copy(s, d).wait_send()
            kg_copy(s, d).wait_send()
    to_sib.wait_send()
    slope_copy.wait_send()
    for d in range(1, chips):
        chip_copy(d).wait_send()
    for d in range(1, zdev):
        mk_copy(d).wait_send()


def shards(sizes, mask_levels, blend_weights, zone_pairs, kernels, resist_cot):
    tiles, zdev, n, rows, zones = sizes
    back, fore = stacked_tables(n)
    zrows = n // zdev
    chips = zdev // CORES
    half = n // CORES
    vmem = pl.BlockSpec(memory_space=pltpu.VMEM)
    anywhere = pl.BlockSpec(memory_space=pl.ANY)
    dma = pltpu.SemaphoreType.DMA
    away = max(tiles - 1, 1)
    mask_grad, kernel_grad = pl.pallas_call(
        functools.partial(kernel, sizes),
        out_shape=(
            jax.ShapeDtypeStruct((zrows, n), F32),
            jax.ShapeDtypeStruct((zones, 1, 2, rows, n), F32),
        ),
        in_specs=[
            pl.BlockSpec(memory_space=pltpu.SMEM),
            vmem,
            vmem,
            anywhere,
            anywhere,
            anywhere,
            anywhere,
        ],
        out_specs=(vmem, vmem),
        scratch_shapes=[
            pltpu.VMEM((n, n), jnp.int32),
            pltpu.VMEM((n, n), F32),
            pltpu.VMEM((2 * n, 2 * n), BF16),
            pltpu.VMEM((2 * n, 2 * n), BF16),
            pltpu.VMEM((tiles, 2, 2, rows, n), BF16),
            pltpu.VMEM((2, 2, n, n), BF16),
            pltpu.VMEM((n, n), BF16),
            pltpu.VMEM((n, 2 * n), BF16),
            pltpu.VMEM((n, 2 * n), F32),
            pltpu.VMEM((2 * n, n), BF16),
            pltpu.VMEM((2, n, 2 * n), F32),
            pltpu.VMEM((n, n), F32),
            pltpu.VMEM((half, n), F32),
            pltpu.VMEM((half, n), F32),
            pltpu.VMEM((chips - 1, half, n), F32),
            pltpu.VMEM((n, n), F32),
            pltpu.VMEM((tiles, 2, 2, rows, n), BF16),
            pltpu.VMEM((tiles, 2, 2, rows, n), BF16),
            pltpu.VMEM((n, 2 * n), F32),
            pltpu.VMEM((2 * n, n), BF16),
            pltpu.VMEM((zrows, n), F32),
            pltpu.VMEM((zdev, zrows, n), BF16),
            pltpu.VMEM((zdev - 1, zrows, n), BF16),
            dma((4,)),
            dma((2, away)),
            dma((2, away)),
            dma,
            dma,
            dma((chips - 1,)),
            dma((chips - 1,)),
            dma,
            dma,
            dma((2, away)),
            dma((2, away)),
            dma((zdev - 1,)),
            dma((zdev - 1,)),
        ],
        compiler_params=pltpu.CompilerParams(
            collective_id=0, has_side_effects=True, vmem_limit_bytes=56 * 1024 * 1024
        ),
        cost_estimate=pl.CostEstimate(
            flops=88 * n * n * n, bytes_accessed=10 * n * n * 4, transcendentals=n * n
        ),
    )(
        zone_pairs,
        blend_weights,
        kernels,
        mask_levels[0],
        resist_cot[0],
        jnp.asarray(back),
        jnp.asarray(fore),
    )
    return (mask_grad[None], kernel_grad)


def solution(mesh):
    placed = (
        P(("grp", "tile"), None, None),
        P(("grp", "tile"), None),
        P("grp", None),
        P(None, "zone", None, "tile", None),
        P(("grp", "tile"), None, None),
    )

    def run(mask_levels, blend_weights, zone_pairs, kernels, resist_cot):
        tiles, zdev = mesh.shape["tile"], mesh.shape["zone"]
        sizes = (
            tiles,
            zdev,
            mask_levels.shape[2],
            kernels.shape[3] // tiles,
            kernels.shape[0],
        )
        return jax.shard_map(
            functools.partial(shards, sizes),
            mesh=mesh,
            in_specs=placed,
            out_specs=(P(("grp", "tile"), "zone", None), P("grp", "zone", None, "tile", None)),
            check_vma=False,
        )(mask_levels, blend_weights, zone_pairs, kernels, resist_cot)

    return run
```

profile of v0, /device:TPU:0, one launch (start us, length us, event | category | flops | bytes accessed | tf_op | source)
XLA Modules:
  0.0 130.7 jit_solution(2733440839041766231)
XLA Ops:
  0.6 1.3 %copy.9.pairs = s32[4,2]{1,0:T(4,128)} copy(s32[4,2]{0,1:T(2,128)} %param.9) | data formatting | bytes 64 | tf_op args[2]
  2.0 124.0 %shard_map.86 = (f32[128,512]{1,0:T(8,128)}, f32[4,1,2,128,512]{4,3,2,1,0:T(8,128)}) custom-call(s32[4,2]{1,0:T(4,128)} %copy.9.pairs, s32[1,512]{1,0:T(1,128)} %blend.1, bf16[4,1,2,128,512]{4,3,2,1,0:T(8,128)(2,1)} %kern.1, s32[512,512]{1,0:T(8,128)} %bitcast.4, f32[512,512]{1,0:T(8,128)} %bitcast.5, bf16[1024,1024]{1,0:T(8,128)(2,1)} %constant.4.clone.back_any, ...), custom_call_target="tpu_custom_call" | custom-call | flops 11811160064 | bytes 10485760 | tf_op jit(solution)/shard_map/pallas_call | solution.py:384
  125.9 1.7 %copy.12 = f32[1,128,512]{2,1,0:T(8,128)} copy(f32[1,128,512]{2,1,0:T(8,128)} %bitcast.3) | data formatting | bytes 524288
  127.6 3.1 %copy.13 = f32[4,1,2,128,512]{4,3,2,1,0:T(8,128)} copy(f32[4,1,2,128,512]{4,3,2,1,0:T(8,128)} %get-tuple-element.9) | data formatting | bytes 4194304
where the time goes:
time: 131 us
  Pallas kernels  124 us (95%)
  local copies, waits for them, and re-layouts  6.09 us (5%)
    pallas_call x1, Pallas kernels, shards(): pl.pallas_call(functools.partial(kernel, sizes), out_shape=(jax.ShapeDtyp...  124 us
    unnamed x3, local copies, waits for them, and re-layouts  6.09 us

commit v1 on v0

--- a/solution.py
+++ b/solution.py
@@ -17,6 +17,7 @@
 F32 = jnp.float32
 BF16 = jnp.bfloat16
 MESH = pl.DeviceIdType.MESH
+PIECES = 4
 CORES = 2
 
 
@@ -53,7 +54,7 @@
     back_any,
     fore_any,
     mask_out,
-    kgrad_out,
+    kg_out,
     levels,
     cot,
     back,
@@ -68,6 +69,7 @@
     image,
     sib_in,
     chip_sum,
+    chip_send,
     chip_in,
     slope,
     kg_send,
@@ -90,6 +92,7 @@
     kg_r,
     mk_s,
     mk_r,
+    out_sem,
 ):
     tiles, zdev, length, rows, zones = sizes
     n = length
@@ -172,6 +175,17 @@
 
         blocks(n, step, stage)
 
+    half = n // CORES
+    piece = half // PIECES
+    to_sib = pltpu.make_async_remote_copy(
+        src_ref=image.at[pl.ds(pl.multiple_of((1 - core) * half, half), half), :],
+        dst_ref=sib_in,
+        send_sem=sib_s,
+        recv_sem=sib_r,
+        device_id={"zone": sib},
+        device_id_type=MESH,
+    )
+
     for s in range(2):
         for d in range(1, tiles):
             panel_copy(s, d).wait_recv()
@@ -187,67 +201,64 @@
         from_left(back, 0)
         from_left(back, 1)
 
-        def stage(r, s=s):
-            at = pl.ds(r, step)
+        for i in range(CORES):
+            start = (1 - core) * half if i == 0 else core * half
+            at = pl.ds(pl.multiple_of(start, half), half)
             e = dot(left[at, :], fore[...])
             fields[s, at, :] = e
             er, ei = e[:, :n], e[:, n:]
             term = shares[s] * (er * er + ei * ei)
             image[at, :] = term if s == 0 else image[at, :] + term
-
-        blocks(n, step, stage)
-
-    half = n // CORES
-    mine = pl.ds(pl.multiple_of(core * half, half), half)
-    other = pl.ds(pl.multiple_of((1 - core) * half, half), half)
-    to_sib = pltpu.make_async_remote_copy(
-        src_ref=image.at[other, :],
-        dst_ref=sib_in,
-        send_sem=sib_s,
-        recv_sem=sib_r,
-        device_id={"zone": sib},
-        device_id_type=MESH,
-    )
-    to_sib.start()
+            if s == 1 and i == 0:
+                to_sib.start()
+
     to_sib.wait_recv()
-    chip_sum[...] = image[mine, :] + sib_in[...]
-
-    def chip_copy(d):
+
+    def chip_copy(d, p):
+        at = pl.ds(p * piece, piece)
         return pltpu.make_async_remote_copy(
-            src_ref=chip_sum,
-            dst_ref=chip_in.at[d - 1],
-            send_sem=chip_s.at[d - 1],
-            recv_sem=chip_r.at[d - 1],
+            src_ref=chip_send.at[at, :],
+            dst_ref=chip_in.at[d - 1, at, :],
+            send_sem=chip_s.at[d - 1, p],
+            recv_sem=chip_r.at[d - 1, p],
             device_id={"zone": lax.rem(chip + d, chips) * CORES + core},
             device_id_type=MESH,
         )
 
-    for d in range(1, chips):
-        chip_copy(d).start()
+    for p in range(PIECES):
+        at = pl.ds(p * piece, piece)
+        here = pl.ds(pl.multiple_of(core * half + p * piece, piece), piece)
+        total = image[here, :] + sib_in[at, :]
+        chip_sum[at, :] = total
+        chip_send[at, :] = total.astype(BF16)
+        for d in range(1, chips):
+            chip_copy(d, p).start()
     loads[3].wait()
-    for d in range(1, chips):
-        chip_copy(d).wait_recv()
-
-    def stage(r):
-        at = pl.ds(r, 64)
+
+    def slope_copy(p):
+        here = pl.ds(pl.multiple_of(core * half + p * piece, piece), piece)
+        return pltpu.make_async_remote_copy(
+            src_ref=slope.at[here, :],
+            dst_ref=slope.at[here, :],
+            send_sem=slope_s.at[p],
+            recv_sem=slope_r.at[p],
+            device_id={"zone": sib},
+            device_id_type=MESH,
+        )
+
+    for p in range(PIECES):
+        for d in range(1, chips):
+            chip_copy(d, p).wait_recv()
+        at = pl.ds(p * piece, piece)
         total = chip_sum[at, :]
         for d in range(1, chips):
-            total = total + chip_in[d - 1, at, :]
+            total = total + chip_in[d - 1, at, :].astype(F32)
         resist = jax.nn.sigmoid(STEEP * (total - THRESHOLD))
-        here = pl.ds(pl.multiple_of(core * half + r, 64), 64)
+        here = pl.ds(pl.multiple_of(core * half + p * piece, piece), piece)
         slope[here, :] = cot[here, :] * STEEP * resist * (1.0 - resist)
-
-    blocks(half, 64, stage)
-    slope_copy = pltpu.make_async_remote_copy(
-        src_ref=slope.at[mine, :],
-        dst_ref=slope.at[mine, :],
-        send_sem=slope_s,
-        recv_sem=slope_r,
-        device_id={"zone": sib},
-        device_id_type=MESH,
-    )
-    slope_copy.start()
-    slope_copy.wait_recv()
+        slope_copy(p).start()
+    for p in range(PIECES):
+        slope_copy(p).wait_recv()
 
     def kg_copy(s, d):
         peer = lax.rem(me_t + d, tiles)
@@ -341,32 +352,29 @@
         total = total + mk_recv[d - 1].astype(F32)
     mask_out[...] = total
 
-    owners = []
-    for z in range(zones):
-        owner = jnp.int32(0)
-        for t in range(tiles):
-            owner = jnp.where(pairs[t, 0] == z, jnp.int32(t), owner)
-        owners.append(owner)
+    own_slots = pltpu.make_async_copy(kg_recv.at[me_t], kg_out.at[me_t], local_sem.at[4])
+    own_slots.start()
+    stores = [own_slots]
     for s in range(2):
         for d in range(1, tiles):
             kg_copy(s, d).wait_recv()
-    for z in range(zones):
-        own, prior = owners[z], owners[(z - 1) % zones]
-        keep_own = pairs[own, 1] == pairs[own, 0]
-        keep_prior = pairs[prior, 1] != pairs[prior, 0]
-        value = kg_recv[own, 0].astype(F32)
-        value = value + jnp.where(keep_own, kg_recv[own, 1].astype(F32), 0.0)
-        value = value + jnp.where(keep_prior, kg_recv[prior, 1].astype(F32), 0.0)
-        kgrad_out[z, 0] = value
-
+            source = lax.rem(me_t + tiles - d, tiles)
+            store = pltpu.make_async_copy(
+                kg_recv.at[source, s], kg_out.at[source, s], out_sem.at[s, d - 1]
+            )
+            store.start()
+            stores.append(store)
+    for store in stores:
+        store.wait()
     for s in range(2):
         for d in range(1, tiles):
             panel_copy(s, d).wait_send()
             kg_copy(s, d).wait_send()
     to_sib.wait_send()
-    slope_copy.wait_send()
-    for d in range(1, chips):
-        chip_copy(d).wait_send()
+    for p in range(PIECES):
+        slope_copy(p).wait_send()
+        for d in range(1, chips):
+            chip_copy(d, p).wait_send()
     for d in range(1, zdev):
         mk_copy(d).wait_send()
 
@@ -381,11 +389,11 @@
     anywhere = pl.BlockSpec(memory_space=pl.ANY)
     dma = pltpu.SemaphoreType.DMA
     away = max(tiles - 1, 1)
-    mask_grad, kernel_grad = pl.pallas_call(
+    mask_rows, returned = pl.pallas_call(
         functools.partial(kernel, sizes),
         out_shape=(
             jax.ShapeDtypeStruct((zrows, n), F32),
-            jax.ShapeDtypeStruct((zones, 1, 2, rows, n), F32),
+            jax.ShapeDtypeStruct((tiles, 2, 2, rows, n), BF16),
         ),
         in_specs=[
             pl.BlockSpec(memory_space=pltpu.SMEM),
@@ -396,7 +404,7 @@
             anywhere,
             anywhere,
         ],
-        out_specs=(vmem, vmem),
+        out_specs=(vmem, anywhere),
         scratch_shapes=[
             pltpu.VMEM((n, n), jnp.int32),
             pltpu.VMEM((n, n), F32),
@@ -412,7 +420,8 @@
             pltpu.VMEM((n, n), F32),
             pltpu.VMEM((half, n), F32),
             pltpu.VMEM((half, n), F32),
-            pltpu.VMEM((chips - 1, half, n), F32),
+            pltpu.VMEM((half, n), BF16),
+            pltpu.VMEM((chips - 1, half, n), BF16),
             pltpu.VMEM((n, n), F32),
             pltpu.VMEM((tiles, 2, 2, rows, n), BF16),
             pltpu.VMEM((tiles, 2, 2, rows, n), BF16),
@@ -421,19 +430,20 @@
             pltpu.VMEM((zrows, n), F32),
             pltpu.VMEM((zdev, zrows, n), BF16),
             pltpu.VMEM((zdev - 1, zrows, n), BF16),
-            dma((4,)),
+            dma((5,)),
             dma((2, away)),
             dma((2, away)),
             dma,
             dma,
-            dma((chips - 1,)),
-            dma((chips - 1,)),
-            dma,
-            dma,
+            dma((chips - 1, PIECES)),
+            dma((chips - 1, PIECES)),
+            dma((PIECES,)),
+            dma((PIECES,)),
             dma((2, away)),
             dma((2, away)),
             dma((zdev - 1,)),
             dma((zdev - 1,)),
+            dma((2, away)),
         ],
         compiler_params=pltpu.CompilerParams(
             collective_id=0, has_side_effects=True, vmem_limit_bytes=56 * 1024 * 1024
@@ -450,7 +460,52 @@
         jnp.asarray(back),
         jnp.asarray(fore),
     )
-    return (mask_grad[None], kernel_grad)
+    def own_of(zone, pairs):
+        owner = jnp.int32(0)
+        for t in range(tiles):
+            owner = jnp.where(pairs[t, 0] == zone, jnp.int32(t), owner)
+        return owner
+
+    def prior_of(zone, pairs):
+        return own_of(lax.rem(zone + zones - 1, zones), pairs)
+
+    def gather(pairs, mask_in, first, second, earlier, mask_out, kgrad_out):
+        zone = pl.program_id(0)
+        own, prior = own_of(zone, pairs), prior_of(zone, pairs)
+        keep_own = pairs[own, 1] == pairs[own, 0]
+        keep_prior = pairs[prior, 1] != pairs[prior, 0]
+        value = first[0, 0].astype(F32)
+        value = value + jnp.where(keep_own, second[0, 0].astype(F32), 0.0)
+        value = value + jnp.where(keep_prior, earlier[0, 0].astype(F32), 0.0)
+        kgrad_out[0, 0] = value
+
+        @pl.when(zone == 0)
+        def _():
+            mask_out[0] = mask_in[...]
+
+    slot = (1, 1, 2, rows, n)
+    mask_grad, kernel_grad = pl.pallas_call(
+        gather,
+        grid_spec=pltpu.PrefetchScalarGridSpec(
+            num_scalar_prefetch=1,
+            grid=(zones,),
+            in_specs=[
+                pl.BlockSpec((zrows, n), lambda z, pairs: (0, 0)),
+                pl.BlockSpec(slot, lambda z, pairs: (own_of(z, pairs), 0, 0, 0, 0)),
+                pl.BlockSpec(slot, lambda z, pairs: (own_of(z, pairs), 1, 0, 0, 0)),
+                pl.BlockSpec(slot, lambda z, pairs: (prior_of(z, pairs), 1, 0, 0, 0)),
+            ],
+            out_specs=(
+                pl.BlockSpec((1, zrows, n), lambda z, pairs: (0, 0, 0)),
+                pl.BlockSpec((1, 1, 2, rows, n), lambda z, pairs: (z, 0, 0, 0, 0)),
+            ),
+        ),
+        out_shape=(
+            jax.ShapeDtypeStruct((1, zrows, n), F32),
+            jax.ShapeDtypeStruct((zones, 1, 2, rows, n), F32),
+        ),
+    )(zone_pairs, mask_rows, returned, returned, returned)
+    return (mask_grad, kernel_grad)
 
 
 def solution(mesh):

time: 131 us -> 125 us (0.954)
  local copies, waits for them, and re-layouts: 6.09 us -> 1.35 us
    pallas_call x1, Pallas kernels: 124 us -> 117 us  [shards(): pl.pallas_call(functools.partial(kernel, sizes), out_shape=(jax.ShapeDtyp...]
    pallas_call x0 -> x1, Pallas kernels: none -> 5.11 us  [shards(): pl.pallas_call(gather, grid_spec=pltpu.PrefetchScalarGridSpec(num_scalar_...]
    unnamed x3 -> x1, local copies, waits for them, and re-layouts: 6.09 us -> 1.35 us
where the time goes in v1:
time: 125 us
  Pallas kernels  123 us (98%)
  local copies, waits for them, and re-layouts  1.35 us (1%)
    pallas_call x1, Pallas kernels, shards(): pl.pallas_call(functools.partial(kernel, sizes), out_shape=(jax.ShapeDtyp...  117 us
    pallas_call x1, Pallas kernels, shards(): pl.pallas_call(gather, grid_spec=pltpu.PrefetchScalarGridSpec(num_scalar_...  5.11 us

profile of v1, /device:TPU:0, one launch (start us, length us, event | category | flops | bytes accessed | tf_op | source)
XLA Modules:
  0.0 124.5 jit_solution(965443171541842709)
XLA Ops:
  0.6 1.3 %copy.10.pairs = s32[4,2]{1,0:T(4,128)} copy(s32[4,2]{0,1:T(2,128)} %param.9) | data formatting | bytes 64 | tf_op args[2]
  2.0 117.4 %shard_map.86 = (f32[128,512]{1,0:T(8,128)}, bf16[4,2,2,128,512]{4,3,2,1,0:T(8,128)(2,1)}) custom-call(s32[4,2]{1,0:T(4,128)} %copy.10.pairs, s32[1,512]{1,0:T(1,128)} %blend.1, bf16[4,1,2,128,512]{4,3,2,1,0:T(8,128)(2,1)} %kern.1, s32[512,512]{1,0:T(8,128)} %bitcast.2, f32[512,512]{1,0:T(8,128)} %bitcast.3, bf16[1024,1024]{1,0:T(8,128)(2,1)} %constant.4.clone.back_any, ...), custom_call_target="tpu_custom_call" | custom-call | flops 11811160064 | bytes 10485760 | tf_op jit(solution)/shard_map/pallas_call | solution.py:392
  119.4 5.1 %shard_map.87 = (f32[1,128,512]{2,1,0:T(8,128)}, f32[4,1,2,128,512]{4,3,2,1,0:T(8,128)}) custom-call(s32[4,2]{1,0:T(4,128)} %copy.10.pairs, f32[128,512]{1,0:T(8,128)} %get-tuple-element.4.mask_in, bf16[4,2,2,128,512]{4,3,2,1,0:T(8,128)(2,1)} %get-tuple-element.5.first.second.earlier, bf16[4,2,2,128,512]{4,3,2,1,0:T(8,128)(2,1)} %get-tuple-element.5.first.second.earlier, ...), custom_call_target="tpu_custom_call" | custom-call | tf_op jit(solution)/shard_map/pallas_call | solution.py:487

commit v2 on v1

--- a/solution.py
+++ b/solution.py
@@ -139,9 +139,8 @@
             device_id_type=MESH,
         )
 
-    for s in range(2):
-        for d in range(tiles - 1, 0, -1):
-            panel_copy(s, d).start()
+    for d in range(tiles - 1, 0, -1):
+        panel_copy(0, d).start()
     for load in loads:
         load.start()
 
@@ -186,6 +185,9 @@
         device_id_type=MESH,
     )
 
+    for d in range(tiles - 1, 0, -1):
+        panel_copy(0, d).wait_send()
+        panel_copy(1, d).start()
     for s in range(2):
         for d in range(1, tiles):
             panel_copy(s, d).wait_recv()
@@ -368,8 +370,9 @@
         store.wait()
     for s in range(2):
         for d in range(1, tiles):
-            panel_copy(s, d).wait_send()
             kg_copy(s, d).wait_send()
+    for d in range(1, tiles):
+        panel_copy(1, d).wait_send()
     to_sib.wait_send()
     for p in range(PIECES):
         slope_copy(p).wait_send()
@@ -466,45 +469,28 @@
             owner = jnp.where(pairs[t, 0] == zone, jnp.int32(t), owner)
         return owner
 
-    def prior_of(zone, pairs):
-        return own_of(lax.rem(zone + zones - 1, zones), pairs)
-
-    def gather(pairs, mask_in, first, second, earlier, mask_out, kgrad_out):
-        zone = pl.program_id(0)
-        own, prior = own_of(zone, pairs), prior_of(zone, pairs)
-        keep_own = pairs[own, 1] == pairs[own, 0]
-        keep_prior = pairs[prior, 1] != pairs[prior, 0]
-        value = first[0, 0].astype(F32)
-        value = value + jnp.where(keep_own, second[0, 0].astype(F32), 0.0)
-        value = value + jnp.where(keep_prior, earlier[0, 0].astype(F32), 0.0)
-        kgrad_out[0, 0] = value
-
-        @pl.when(zone == 0)
-        def _():
-            mask_out[0] = mask_in[...]
-
-    slot = (1, 1, 2, rows, n)
+    def gather(pairs, mask_in, got, mask_out, kgrad_out):
+        mask_out[0] = mask_in[...]
+        for zone in range(zones):
+            own, prior = own_of(zone, pairs), own_of((zone - 1) % zones, pairs)
+            keep_own = pairs[own, 1] == pairs[own, 0]
+            keep_prior = pairs[prior, 1] != pairs[prior, 0]
+            for c in range(2):
+                value = got[own, 0, c].astype(F32)
+                value = value + jnp.where(keep_own, got[own, 1, c].astype(F32), 0.0)
+                value = value + jnp.where(keep_prior, got[prior, 1, c].astype(F32), 0.0)
+                kgrad_out[zone, 0, c] = value
+
     mask_grad, kernel_grad = pl.pallas_call(
         gather,
-        grid_spec=pltpu.PrefetchScalarGridSpec(
-            num_scalar_prefetch=1,
-            grid=(zones,),
-            in_specs=[
-                pl.BlockSpec((zrows, n), lambda z, pairs: (0, 0)),
-                pl.BlockSpec(slot, lambda z, pairs: (own_of(z, pairs), 0, 0, 0, 0)),
-                pl.BlockSpec(slot, lambda z, pairs: (own_of(z, pairs), 1, 0, 0, 0)),
-                pl.BlockSpec(slot, lambda z, pairs: (prior_of(z, pairs), 1, 0, 0, 0)),
-            ],
-            out_specs=(
-                pl.BlockSpec((1, zrows, n), lambda z, pairs: (0, 0, 0)),
-                pl.BlockSpec((1, 1, 2, rows, n), lambda z, pairs: (z, 0, 0, 0, 0)),
-            ),
-        ),
+        in_specs=[pl.BlockSpec(memory_space=pltpu.SMEM), vmem, vmem],
+        out_specs=(vmem, vmem),
         out_shape=(
             jax.ShapeDtypeStruct((1, zrows, n), F32),
             jax.ShapeDtypeStruct((zones, 1, 2, rows, n), F32),
         ),
-    )(zone_pairs, mask_rows, returned, returned, returned)
+        compiler_params=pltpu.CompilerParams(vmem_limit_bytes=60 * 1024 * 1024),
+    )(zone_pairs, mask_rows, returned)
     return (mask_grad, kernel_grad)
 
 

time: 125 us -> 123 us (0.984)
  Pallas kernels: 123 us -> 121 us
    pallas_call x1, Pallas kernels: 5.11 us -> 3.51 us  [shards(): pl.pallas_call(gather, in_specs=[pl.BlockSpec(memory_space=pltpu.SMEM), v...]
where the time goes in v2:
time: 123 us
  Pallas kernels  121 us (98%)
  local copies, waits for them, and re-layouts  1.35 us (1%)
    pallas_call x1, Pallas kernels, shards(): pl.pallas_call(functools.partial(kernel, sizes), out_shape=(jax.ShapeDtyp...  117 us
    pallas_call x1, Pallas kernels, shards(): pl.pallas_call(gather, in_specs=[pl.BlockSpec(memory_space=pltpu.SMEM), v...  3.51 us

profile of v2, /device:TPU:0, one launch (start us, length us, event | category | flops | bytes accessed | tf_op | source)
XLA Modules:
  0.0 122.9 jit_solution(13024246210315324633)
XLA Ops:
  0.6 1.3 %copy.10.pairs = s32[4,2]{1,0:T(4,128)} copy(s32[4,2]{0,1:T(2,128)} %param.9) | data formatting | bytes 64 | tf_op args[2]
  2.0 117.4 %shard_map.86 = (f32[128,512]{1,0:T(8,128)}, bf16[4,2,2,128,512]{4,3,2,1,0:T(8,128)(2,1)}) custom-call(s32[4,2]{1,0:T(4,128)} %copy.10.pairs, s32[1,512]{1,0:T(1,128)} %blend.1, bf16[4,1,2,128,512]{4,3,2,1,0:T(8,128)(2,1)} %kern.1, s32[512,512]{1,0:T(8,128)} %bitcast.2, f32[512,512]{1,0:T(8,128)} %bitcast.3, bf16[1024,1024]{1,0:T(8,128)(2,1)} %constant.4.clone.back_any, ...), custom_call_target="tpu_custom_call" | custom-call | flops 11811160064 | bytes 10485760 | tf_op jit(solution)/shard_map/pallas_call | solution.py:395
  119.4 3.5 %shard_map.87 = (f32[1,128,512]{2,1,0:T(8,128)}, f32[4,1,2,128,512]{4,3,2,1,0:T(8,128)}) custom-call(s32[4,2]{1,0:T(4,128)} %copy.10.pairs, f32[128,512]{1,0:T(8,128)} %get-tuple-element.4.mask_in, bf16[4,2,2,128,512]{4,3,2,1,0:T(8,128)(2,1)} %get-tuple-element.5.got), custom_call_target="tpu_custom_call" | custom-call | tf_op jit(solution)/shard_map/pallas_call | solution.py:484

commit v3 on v2

--- a/solution.py
+++ b/solution.py
@@ -17,7 +17,7 @@
 F32 = jnp.float32
 BF16 = jnp.bfloat16
 MESH = pl.DeviceIdType.MESH
-PIECES = 4
+PIECES = 2
 CORES = 2
 
 
@@ -303,7 +303,7 @@
             return (vr * sr + vi * si).astype(BF16), (vi * sr - vr * si).astype(BF16)
 
         def away(i, carry, s=s):
-            d = tiles - 1 - i
+            d = (tiles // 2 + i - 1) % (tiles - 1) + 1
             peer = lax.rem(me_t + d, tiles)
             re, im = rows_of(peer)
             kg_send[peer, s, 0] = re

time: 123 us -> 119 us (0.967)
  the two profiles are of different devices: /device:TPU:0 before, /device:TPU:9 now
where the time goes in v3:
time: 119 us
  Pallas kernels  117 us (98%)
  local copies, waits for them, and re-layouts  1.35 us (1%)
    pallas_call x1, Pallas kernels, shards(): pl.pallas_call(functools.partial(kernel, sizes), out_shape=(jax.ShapeDtyp...  113 us
    pallas_call x1, Pallas kernels, shards(): pl.pallas_call(gather, in_specs=[pl.BlockSpec(memory_space=pltpu.SMEM), v...  3.51 us

profile of v3, /device:TPU:9, one launch (start us, length us, event | category | flops | bytes accessed | tf_op | source)
XLA Modules:
  0.0 118.9 jit_solution(15530619488423535898)
XLA Ops:
  0.6 1.3 %copy.10.pairs = s32[4,2]{1,0:T(4,128)} copy(s32[4,2]{0,1:T(2,128)} %param.9) | data formatting | bytes 64 | tf_op args[2]
  2.0 113.4 %shard_map.86 = (f32[128,512]{1,0:T(8,128)}, bf16[4,2,2,128,512]{4,3,2,1,0:T(8,128)(2,1)}) custom-call(s32[4,2]{1,0:T(4,128)} %copy.10.pairs, s32[1,512]{1,0:T(1,128)} %blend.1, bf16[4,1,2,128,512]{4,3,2,1,0:T(8,128)(2,1)} %kern.1, s32[512,512]{1,0:T(8,128)} %bitcast.2, f32[512,512]{1,0:T(8,128)} %bitcast.3, bf16[1024,1024]{1,0:T(8,128)(2,1)} %constant.4.clone.back_any, ...), custom_call_target="tpu_custom_call" | custom-call | flops 11811160064 | bytes 10485760 | tf_op jit(solution)/shard_map/pallas_call | solution.py:395
  115.3 3.5 %shard_map.87 = (f32[1,128,512]{2,1,0:T(8,128)}, f32[4,1,2,128,512]{4,3,2,1,0:T(8,128)}) custom-call(s32[4,2]{1,0:T(4,128)} %copy.10.pairs, f32[128,512]{1,0:T(8,128)} %get-tuple-element.4.mask_in, bf16[4,2,2,128,512]{4,3,2,1,0:T(8,128)(2,1)} %get-tuple-element.5.got), custom_call_target="tpu_custom_call" | custom-call | tf_op jit(solution)/shard_map/pallas_call | solution.py:484
